TPU v7x, 256 devices: a whole 4x4x8 slice. The times are simulated.
256 devices in a mesh: dp: 4 (over x), section: 2 (over z_hi), shard: 32 (over z_lo, y, core).
Axes of the slice: x: 4, y: 4, z: 8 (z_hi: 2, z_lo: 4; z = z_hi * 4 + z_lo), core: 2. Of those that a mesh axis runs over, the one named last changes fastest.
Arguments:
- projections: bfloat16 [2, 8, 2048, 3, 4096], P('section', 'dp', 'shard'), may hold values from -40 to 40
- bias_terms: float32 [3, 4096], replicated, may hold values from -3 to 3
- context_grad: bfloat16 [2, 4, 32, 1, 2048, 256], P('section', 'dp', 'shard'), may hold values from -20 to 20
Outputs:
- context: bfloat16 [2, 4, 32, 1, 2048, 256], P('section', 'dp', 'shard')
- projection_grad: bfloat16 [2, 8, 2048, 3, 4096], P('section', 'dp', 'shard')
- bias_grad: float32 [3, 4096], replicated
All inputs are finite; a program needn't handle non-finite values.
Results may differ from a plain program's by a relative error of at most 0.012.
The roundings to bfloat16 on the way count: a program that leaves them out, or rounds other values in their place, can miss the bound.
Values may be sent and summed in bfloat16 or wider, within the bound.
A program may use at most 128 MiB of HBM per device.

v0:
```python
import jax
import jax.numpy as jnp
from jax import lax
from jax.sharding import PartitionSpec as P

HEAD_DIM = 128


def partner(x, axis, distance):
    return lax.ppermute(x, axis, [(i, i ^ 1 << distance) for i in range(lax.axis_size(axis))])


def for_sending(x):
    return jax.tree.map(lambda a: a.astype(jnp.bfloat16) if a.dtype == jnp.float32 else a, x)


def attend_sequence(inputs):
    query, keyed, valued, grad_out = inputs
    length = query.shape[0]
    block_rows = min(length, 512)
    score_scale = HEAD_DIM ** (-0.5)
    key_accum = jnp.zeros(keyed.shape, jnp.float32)
    value_accum = jnp.zeros(valued.shape, jnp.float32)
    context_parts = []
    query_parts = []
    for block_id in range(length // block_rows):
        first_row = block_id * block_rows
        last_row = first_row + block_rows
        query_rows = query[first_row:last_row]
        grad_rows = grad_out[first_row:last_row]
        key_rows = keyed[:last_row]
        value_rows = valued[:last_row]
        scores = (
            jnp.einsum("qhd,khd->hqk", query_rows, key_rows, preferred_element_type=jnp.float32)
            * score_scale
        )
        row_ids = first_row + lax.broadcasted_iota(jnp.int32, (block_rows, last_row), 0)
        col_ids = lax.broadcasted_iota(jnp.int32, (block_rows, last_row), 1)
        scores = jnp.where(col_ids <= row_ids, scores, -jnp.inf)
        row_top = jnp.max(scores, axis=2, keepdims=True)
        exponent = jnp.exp(scores - row_top)
        probability = exponent / jnp.sum(exponent, axis=2, keepdims=True)
        weights = probability.astype(jnp.bfloat16)
        context_parts.append(
            jnp.einsum(
                "hqk,khd->qhd", weights, value_rows, preferred_element_type=jnp.float32
            ).astype(jnp.bfloat16)
        )
        grad_prob = jnp.einsum(
            "qhd,khd->hqk", grad_rows, value_rows, preferred_element_type=jnp.float32
        )
        row_delta = jnp.sum(probability * grad_prob, axis=2, keepdims=True)
        grad_score = (probability * (grad_prob - row_delta) * score_scale).astype(jnp.bfloat16)
        query_parts.append(
            jnp.einsum(
                "hqk,khd->qhd", grad_score, key_rows, preferred_element_type=jnp.float32
            ).astype(jnp.bfloat16)
        )
        key_accum = key_accum.at[:last_row].add(
            jnp.einsum("hqk,qhd->khd", grad_score, query_rows, preferred_element_type=jnp.float32)
        )
        value_accum = value_accum.at[:last_row].add(
            jnp.einsum("hqk,qhd->khd", weights, grad_rows, preferred_element_type=jnp.float32)
        )
    context = jnp.concatenate(context_parts, axis=0)
    grad_query = jnp.concatenate(query_parts, axis=0)
    return (context, grad_query, key_accum.astype(jnp.bfloat16), value_accum.astype(jnp.bfloat16))


def per_device(projections, bias_terms, context_grad):
    shards = lax.axis_size("shard")
    groups = shards // 2
    local_rows = projections[0]
    batch_count, piece_length, triple, width_all = local_rows.shape
    half_batch = batch_count // 2
    head_width = width_all // groups
    per_head = head_width // HEAD_DIM
    full_length = shards * piece_length
    biased = (local_rows.astype(jnp.float32) + bias_terms).astype(jnp.bfloat16)
    outbound = biased.reshape(2, half_batch, piece_length, 3, groups, head_width)
    outbound = outbound.transpose(0, 4, 1, 2, 3, 5).reshape(
        shards, half_batch, piece_length, 3, head_width
    )
    crossed = partner(outbound, "section", 0)
    arrived = lax.all_to_all(crossed, "shard", split_axis=0, concat_axis=0, tiled=True)
    head_layout = arrived.transpose(1, 0, 2, 3, 4).reshape(
        half_batch, full_length, 3, per_head, HEAD_DIM
    )
    grad_out = context_grad.reshape(half_batch, full_length, per_head, HEAD_DIM)
    context, grad_query, grad_key, grad_value = lax.map(
        attend_sequence,
        (head_layout[:, :, 0], head_layout[:, :, 1], head_layout[:, :, 2], grad_out),
    )
    gradients = jnp.stack((grad_query, grad_key, grad_value), axis=2).reshape(
        half_batch, full_length, 3, head_width
    )
    returning = gradients.reshape(half_batch, shards, piece_length, 3, head_width).transpose(
        1, 0, 2, 3, 4
    )
    out_context = context.reshape(1, 1, 1, half_batch, full_length, head_width)
    regathered = lax.all_to_all(
        for_sending(returning), "shard", split_axis=0, concat_axis=0, tiled=True
    ).astype(returning.dtype)
    returned = partner(for_sending(regathered), "section", 0).astype(regathered.dtype)
    seq_grads = returned.reshape(2, groups, half_batch, piece_length, 3, head_width)
    seq_grads = seq_grads.transpose(0, 2, 3, 4, 1, 5).reshape(
        batch_count, piece_length, 3, width_all
    )
    bias_total = lax.psum(
        jnp.sum(seq_grads.astype(jnp.float32), axis=(0, 1)), ("dp", "section", "shard")
    )
    return (out_context, seq_grads[None], bias_total)


def solution(mesh):
    placed = (
        P("section", "dp", "shard", None, None),
        P(),
        P("section", "dp", "shard", None, None, None),
    )
    return jax.shard_map(
        per_device,
        mesh=mesh,
        in_specs=placed,
        out_specs=(
            P("section", "dp", "shard", None, None, None),
            P("section", "dp", "shard", None, None),
            P(),
        ),
        check_vma=False,
    )
```

profile of v0, /device:TPU:1, one launch (start us, length us, event | category | flops | bytes accessed | tf_op | source)
XLA Modules:
  0.0 732.5 jit_solution(5063346200876814826)
XLA Ops:
  1.5 2.6 convert_element_type.153
  4.1 2.8 copy.284
  9.1 7.8 %collective-permute-start = (bf16[32,1,64,3,256]{4,2,3,1,0:T(8,128)(2,1)S(1)}, bf16[32,1,64,3,256]{4,2,3,1,0:T(8,128)(2,1)}, u32[]{:S(2)}, u32[]{:S(2)}) collective-permute-start(bf16[32,1,64,3,256]{4,2,3,1,0:T(8,128)(2,1)S(1)} %bitcast.333), channel_id=1, source_target_pairs={{0,32},{32,0},{1,33},{33,1},{2,34},{34,2},{3,35},{35,3},{4,36},{36... | collective-permute-start | bytes 9437192 | tf_op jit(solution)/shard_map/ppermute | solution.py:10
  16.9 102.2 %collective-permute-done = bf16[32,1,64,3,256]{4,2,3,1,0:T(8,128)(2,1)} collective-permute-done((bf16[32,1,64,3,256]{4,2,3,1,0:T(8,128)(2,1)S(1)}, bf16[32,1,64,3,256]{4,2,3,1,0:T(8,128)(2,1)}, u32[]{:S(2)}, u32[]{:S(2)}) %collective-permute-start) | collective-permute-done | bytes 3145760 | tf_op jit(solution)/shard_map/ppermute | solution.py:10
  119.1 42.0 %all-to-all-start = ((bf16[32,1,64,3,256]{4,2,3,1,0:T(8,128)(2,1)}), bf16[32,1,64,3,256]{4,2,3,1,0:T(8,128)(2,1)S(1)}, u32[]{:S(2)}, u32[]{:S(2)}) async-start(bf16[32,1,64,3,256]{4,2,3,1,0:T(8,128)(2,1)} %collective-permute-done), calls=%async_computation | async-start | bytes 6291456 | tf_op jit(solution)/shard_map/all_to_all | solution.py:85
  161.1 2.1 fusion.139
  163.2 1.8 copy.283
  165.0 1.8 copy.282
  172.1 1.7 iota_compare_fusion
  173.8 57.8 %all-to-all-done = bf16[32,1,64,3,256]{4,2,3,1,0:T(8,128)(2,1)S(1)} async-done(((bf16[32,1,64,3,256]{4,2,3,1,0:T(8,128)(2,1)}), bf16[32,1,64,3,256]{4,2,3,1,0:T(8,128)(2,1)S(1)}, u32[]{:S(2)}, u32[]{:S(2)}) %all-to-all-start) | async-done | bytes 3145760 | tf_op jit(solution)/shard_map/all_to_all | solution.py:85
  231.6 1.9 copy.187
  233.5 3.8 reshape_transpose.3
  237.2 1.7 fusion.136
  238.9 2.0 fusion.135
  241.0 2.0 fusion.137
  243.0 2.4 fusion.138
  247.0 3.9 fusion.143
  251.0 2.9 convolution_bitcast_fusion.3
  253.9 4.0 fusion.81
  257.8 5.5 convolution_bitcast_fusion.4
  265.8 3.0 scatter-add.20
  268.8 2.6 scatter-add.25
  271.4 2.7 fusion.101
  274.8 3.8 fusion.142
  278.7 13.1 %fusion.76 = bf16[512,2,128]{0,2,1:T(8,128)(2,1)} fusion(f32[2,1024,512]{1,2,0:T(8,128)} %fusion.101, bf16[1,1024,1,2,128]{4,3,1,2,0:T(2,128)(2,1)S(1)} %copy-done.13, f32[2,512,1024]{2,1,0:T(8,128)} %get-tuple-element.218, f32[2,512]{1,0:T(2,128)S(1)} %get-tuple-element.217), kind=kOutput, calls=%fused_computation.105 | convolution fusion | flops 275908608 | bytes 9179136 | tf_op jit(solution)/shard_map/while/body/eval_jaxpr/hqk,khd->qhd/dot_general | solution.py:55
  291.7 10.8 %fusion.63 = f32[2048,2,128]{0,2,1:T(8,128)} fusion(f32[2048,2,128]{0,2,1:T(8,128)} %scatter-add.20, f32[2,1024,512]{1,2,0:T(8,128)} %fusion.101, bf16[1,512,1,2,128]{4,3,1,2,0:T(2,128)(2,1)S(1)} %copy-done.16, f32[2,512,1024]{2,1,0:T(8,128)} %get-tuple-element.218, f32[2,512]{1,0:T(2,128)S(1)} %get-tuple-element.217), kind=kOutput, calls=%fused_computation.91 | convolution fusion | flops 276039680 | bytes 19144704 | tf_op jit(solution)/shard_map/while/body/eval_jaxpr/hqk,qhd->khd/dot_general | solution.py:60
  302.5 4.5 fusion.61
  307.0 3.7 fusion.97
  310.7 6.5 fusion.141
  317.3 5.5 fusion.37
  322.8 16.8 %fusion.75 = bf16[512,2,128]{0,2,1:T(8,128)(2,1)} fusion(f32[2,1536,512]{1,2,0:T(8,128)} %fusion.97, bf16[1,1536,1,2,128]{4,3,1,2,0:T(2,128)(2,1)} %get-tuple-element.205, f32[2,512,1536]{2,1,0:T(8,128)} %get-tuple-element.216, f32[2,512]{1,0:T(2,128)S(1)} %get-tuple-element.215), kind=kOutput, calls=%fused_computation.104 | convolution fusion | flops 413796864 | bytes 13635584 | tf_op jit(solution)/shard_map/while/body/eval_jaxpr/hqk,khd->qhd/dot_general | solution.py:55
  339.7 16.1 %fusion.39 = f32[2048,2,128]{0,2,1:T(8,128)} fusion(f32[2048,2,128]{0,2,1:T(8,128)} %fusion.63, f32[2,1536,512]{1,2,0:T(8,128)} %fusion.97, bf16[1,512,1,2,128]{4,3,1,2,0:T(2,128)(2,1)} %get-tuple-element.198, f32[2,512,1536]{2,1,0:T(8,128)} %get-tuple-element.216, f32[2,512]{1,0:T(2,128)S(1)} %get-tuple-element.215), kind=kOutput, calls=%fused_computation.60 | convolution fusion | flops 414059008 | bytes 28581888 | tf_op jit(solution)/shard_map/while/body/eval_jaxpr/hqk,qhd->khd/dot_general | solution.py:60
  355.8 4.5 fusion.85
  361.6 8.7 %fusion.140 = (f32[2,512]{1,0:T(2,128)S(1)}, f32[2,512,2048]{2,1,0:T(8,128)}) fusion(f32[2,512,2048]{2,1,0:T(8,128)S(1)} %fusion.96, pred[512,2048]{1,0:T(8,128)(4,1)} %iota_compare_fusion), kind=kOutput, calls=%fused_computation.180 | output fusion | flops 12584959 | bytes 17829888 | tf_op jit(solution)/shard_map/while/body/eval_jaxpr/sub | solution.py:41
  370.3 18.2 %fusion.74 = bf16[512,2,128]{0,2,1:T(8,128)(2,1)} fusion(f32[2,2048,512]{1,2,0:T(8,128)} %fusion.85, bf16[1,2048,1,2,128]{4,3,1,2,0:T(2,128)(2,1)S(1)} %copy-done.2, f32[2,512,2048]{2,1,0:T(8,128)} %get-tuple-element.214, f32[2,512]{1,0:T(2,128)S(1)} %get-tuple-element.213), kind=kOutput, calls=%fused_computation.103 | convolution fusion | flops 551685120 | bytes 18092032 | tf_op jit(solution)/shard_map/while/body/eval_jaxpr/hqk,khd->qhd/dot_general | solution.py:55
  388.5 15.8 %fusion.42 = bf16[2048,2,128]{0,2,1:T(8,128)(2,1)} fusion(f32[2048,2,128]{0,2,1:T(8,128)} %fusion.39, f32[2,2048,512]{1,2,0:T(8,128)} %fusion.85, bf16[1,512,1,2,128]{4,3,1,2,0:T(2,128)(2,1)S(1)} %copy-done.15, f32[2,512,2048]{2,1,0:T(8,128)} %get-tuple-element.214, f32[2,512]{1,0:T(2,128)S(1)} %get-tuple-element.213), kind=kOutput, calls=%fused_computation.63 | convolution fusion | flops 552602624 | bytes 20189184 | tf_op jit(solution)/shard_map/while/body/eval_jaxpr/hqk,qhd->khd/dot_general | solution.py:60
  404.3 5.2 fusion.41
  409.5 8.7 %copy.235 = bf16[2048,2,128]{2,1,0:T(2,128)(2,1)S(1)} copy(bf16[2048,2,128]{2,0,1:T(8,128)(2,1)S(1)} %fusion.41) | data formatting | bytes 2097152 | tf_op jit(solution)/shard_map/while/body/eval_jaxpr/convert_element_type | solution.py:67
  421.4 2.5 copy.227
  427.4 77.9 %all_to_all.10 = bf16[32,1,64,3,256]{4,2,3,1,0:T(8,128)(2,1)} all-to-all(bf16[32,1,64,3,256]{4,2,3,1,0:T(8,128)(2,1)S(1)} %copy.236), channel_id=1, replica_groups=mesh['dp'=4,'section'=2,'shard'=32] {'shard'}, dimensions={0} | all-to-all | bytes 6291456 | tf_op jit(solution)/shard_map/all_to_all | solution.py:101
  505.3 3.8 collective-permute-start.1
  509.1 5.4 fusion.77
  514.5 2.1 fusion.80
  523.2 2.3 copy.238
  525.5 121.4 %collective-permute-done.1 = bf16[32,1,64,3,256]{4,2,3,1,0:T(8,128)(2,1)S(1)} collective-permute-done((bf16[32,1,64,3,256]{4,2,3,1,0:T(8,128)(2,1)}, bf16[32,1,64,3,256]{4,2,3,1,0:T(8,128)(2,1)S(1)}, u32[]{:S(2)}, u32[]{:S(2)}) %collective-permute-start.1) | collective-permute-done | bytes 3145760 | tf_op jit(solution)/shard_map/ppermute | solution.py:10
  647.5 3.5 copy.237
  651.1 5.9 broadcast_in_dim_reshape.3
  656.9 75.3 %psum.7 = f32[3,4096]{1,0:T(4,128)} all-reduce(f32[3,4096]{1,0:T(4,128)S(1)} %bitcast.342), channel_id=1, replica_groups=mesh['dp'=4,'section'=2,'shard'=32] {'dp','section','shard'}, use_global_device_ids=true, to_apply=%region_13.14 | all-reduce | flops 12288 | bytes 98304 | tf_op jit(solution)/shard_map/psum | solution.py:109
  (96 shorter events, 28.1 us)
Async XLA Ops:
  9.1 110.0 %collective-permute-start = (bf16[32,1,64,3,256]{4,2,3,1,0:T(8,128)(2,1)S(1)}, bf16[32,1,64,3,256]{4,2,3,1,0:T(8,128)(2,1)}, u32[]{:S(2)}, u32[]{:S(2)}) collective-permute-start(bf16[32,1,64,3,256]{4,2,3,1,0:T(8,128)(2,1)S(1)} %bitcast.333), channel_id=1, source_target_pairs={{0,32},{32,0},{1,33},{33,1},{2,34},{34,2},{3,35},{35,3},{4,36},{36... | collective-permute-start | bytes 9437192 | tf_op jit(solution)/shard_map/ppermute | solution.py:10
  119.1 112.5 %all-to-all-start = ((bf16[32,1,64,3,256]{4,2,3,1,0:T(8,128)(2,1)}), bf16[32,1,64,3,256]{4,2,3,1,0:T(8,128)(2,1)S(1)}, u32[]{:S(2)}, u32[]{:S(2)}) async-start(bf16[32,1,64,3,256]{4,2,3,1,0:T(8,128)(2,1)} %collective-permute-done), calls=%async_computation | async-start | bytes 6291456 | tf_op jit(solution)/shard_map/all_to_all | solution.py:85
  246.5 7.3 %copy-start.18 = (bf16[1,512,1,2,128]{1,4,3,2,0:T(8,128)(2,1)}, bf16[1,512,1,2,128]{1,4,3,2,0:T(8,128)(2,1)S(1)}, u32[]{:S(2)}) copy-start(bf16[1,512,1,2,128]{1,4,3,2,0:T(8,128)(2,1)S(1)} %copy.268) | copy-start | bytes 786436
  247.0 6.9 copy-start.7
  251.0 2.9 copy-start.24
  253.9 4.0 copy-start.23
  257.8 5.5 copy-start.14
  257.8 6.0 copy-start.6
  257.8 6.6 copy-start.3
  263.8 7.7 %copy-start.8 = (bf16[1,1024,1,2,128]{1,4,3,2,0:T(8,128)(2,1)}, bf16[1,1024,1,2,128]{1,4,3,2,0:T(8,128)(2,1)S(1)}, u32[]{:S(2)}) copy-start(bf16[1,1024,1,2,128]{1,4,3,2,0:T(8,128)(2,1)S(1)} %copy.271) | copy-start | bytes 1572868
  264.4 42.6 %copy-start.5 = (bf16[1,1536,1,2,128]{1,4,3,2,0:T(8,128)(2,1)}, bf16[1,1536,1,2,128]{1,4,3,2,0:T(8,128)(2,1)S(1)}, u32[]{:S(2)}) copy-start(bf16[1,1536,1,2,128]{1,4,3,2,0:T(8,128)(2,1)S(1)} %copy.274) | copy-start | bytes 2359300
  265.8 90.0 %copy-start = (bf16[1,2048,1,2,128]{1,4,3,2,0:T(8,128)(2,1)}, bf16[1,2048,1,2,128]{1,4,3,2,0:T(8,128)(2,1)S(1)}, u32[]{:S(2)}) copy-start(bf16[1,2048,1,2,128]{1,4,3,2,0:T(8,128)(2,1)S(1)} %copy.277) | copy-start | bytes 3145732
  265.8 5.7 copy-start.21
  268.8 5.3 copy-start.13
  268.8 5.3 copy-start.16
  271.4 3.4 copy-start.22
  302.5 4.5 copy-start.20
  310.7 6.6 copy-start.10
  322.8 16.9 %copy-start.11 = (f32[2048,2,128]{2,0,1:T(8,128)}, f32[2048,2,128]{2,0,1:T(8,128)S(1)}, u32[]{:S(2)}) copy-start(f32[2048,2,128]{2,0,1:T(8,128)S(1)} %fusion.37) | copy-start | bytes 6291460
  339.7 16.2 %copy-start.17 = (bf16[1,1,1,1,512,256]{4,5,3,2,1,0:T(8,128)(2,1)S(1)}, bf16[1,1,1,1,512,256]{4,5,3,2,1,0:T(8,128)(2,1)}, u32[]{:S(2)}) copy-start(bf16[1,1,1,1,512,256]{4,5,3,2,1,0:T(8,128)(2,1)} %copy.283) | copy-start | bytes 786436
  355.8 4.5 copy-start.2
  355.8 4.5 copy-start.15
  388.5 15.8 %copy-start.12 = (f32[2048,2,128]{2,0,1:T(8,128)S(1)}, f32[2048,2,128]{2,0,1:T(8,128)}, u32[]{:S(2)}) copy-start(f32[2048,2,128]{2,0,1:T(8,128)} %copy-done.11) | copy-start | bytes 6291460
  409.5 9.4 %copy-start.25 = (bf16[512,2,128]{0,2,1:T(8,128)(2,1)S(1)}, bf16[512,2,128]{0,2,1:T(8,128)(2,1)}, u32[]{:S(2)}) copy-start(bf16[512,2,128]{0,2,1:T(8,128)(2,1)} %fusion.81) | copy-start | bytes 786436
  409.5 9.4 %copy-start.26 = (bf16[512,2,128]{0,2,1:T(8,128)(2,1)S(1)}, bf16[512,2,128]{0,2,1:T(8,128)(2,1)}, u32[]{:S(2)}) copy-start(bf16[512,2,128]{0,2,1:T(8,128)(2,1)} %fusion.76) | copy-start | bytes 786436
  409.5 9.4 %copy-start.27 = (bf16[512,2,128]{0,2,1:T(8,128)(2,1)S(1)}, bf16[512,2,128]{0,2,1:T(8,128)(2,1)}, u32[]{:S(2)}) copy-start(bf16[512,2,128]{0,2,1:T(8,128)(2,1)} %fusion.75) | copy-start | bytes 786436
  409.5 9.4 %copy-start.29 = (bf16[512,2,128]{0,2,1:T(8,128)(2,1)S(1)}, bf16[512,2,128]{0,2,1:T(8,128)(2,1)}, u32[]{:S(2)}) copy-start(bf16[512,2,128]{0,2,1:T(8,128)(2,1)} %fusion.74) | copy-start | bytes 786436
  421.4 4.0 copy-start.4
  505.3 9.2 %copy-start.19 = (bf16[1,512,1,2,128]{1,4,3,2,0:T(8,128)(2,1)S(1)}, bf16[1,512,1,2,128]{1,4,3,2,0:T(8,128)(2,1)}, u32[]{:S(2)}) copy-start(bf16[1,512,1,2,128]{1,4,3,2,0:T(8,128)(2,1)} %copy-done.18) | copy-start | bytes 786436
  505.3 141.5 %collective-permute-start.1 = (bf16[32,1,64,3,256]{4,2,3,1,0:T(8,128)(2,1)}, bf16[32,1,64,3,256]{4,2,3,1,0:T(8,128)(2,1)S(1)}, u32[]{:S(2)}, u32[]{:S(2)}) collective-permute-start(bf16[32,1,64,3,256]{4,2,3,1,0:T(8,128)(2,1)} %all_to_all.10), channel_id=1, source_target_pairs={{0,32},{32,0},{1,33},{33,1},{2,34},{34,2},{3,35},{35,3},{4,36},{36... | collective-permute-start | bytes 9437192 | tf_op jit(solution)/shard_map/ppermute | solution.py:10
  514.5 2.1 copy-start.9
  514.5 3.0 copy-start.30
  514.5 4.3 slice-start
  517.5 1.7 copy-start.1
  517.5 3.0 slice-start.1
  520.5 1.6 copy-start.28
where the time goes:
time: 739 us; the launch traced here: 732 us
  waiting for transfers between devices  281 us (38%)
  blocking collectives  153 us (21%)
  matrix products  152 us (21%)
  local copies, waits for them, and re-layouts  66.2 us (9%)
  starting transfers between devices  53.6 us (7%)
  other arithmetic  24.7 us (3%)
    ppermute x2, waiting for transfers between devices, partner(): lax.ppermute(x, axis, [(i, i ^ 1 << distance) for i in range(lax.axis_siz...  224 us
    all_to_all x1, blocking collectives, per_device(): lax.all_to_all(for_sending(returning), 'shard', split_axis=0, concat_axis...  77.9 us
    psum x1, blocking collectives, per_device(): lax.psum(jnp.sum(seq_grads.astype(jnp.float32), axis=(0, 1)), ('dp', 'sec...  75.3 us
    all_to_all x1, waiting for transfers between devices, per_device(): lax.all_to_all(crossed, 'shard', split_axis=0, concat_axis=0, tiled=True)  57.8 us
    dot_general x4, matrix products, attend_sequence(): jnp.einsum('hqk,khd->qhd', grad_score, key_rows, preferred_element_type=j...  52 us
    dot_general x4, matrix products, attend_sequence(): jnp.einsum('hqk,qhd->khd', grad_score, query_rows, preferred_element_type...  48.2 us
    all_to_all x1, starting transfers between devices, per_device(): lax.all_to_all(crossed, 'shard', split_axis=0, concat_axis=0, tiled=True)  42 us
    dot_general x4, matrix products, attend_sequence(): jnp.einsum('hqk,qhd->khd', weights, grad_rows, preferred_element_type=jnp...  18.1 us
  transfers between devices with their start and end apart: 3, of which 3 were waited for; matrix products, arithmetic and copies ran while one was open for 4% of the time, Pallas kernels for 0%

commit v1 on v0

v1 whole, which is shorter than its diff:
```python
import functools

import jax
import jax.numpy as jnp
from jax import lax
from jax.experimental import pallas as pl
from jax.experimental.pallas import tpu as pltpu
from jax.sharding import PartitionSpec as P

HEAD_DIM = 128
N_Z, N_Y, N_CORE = 4, 4, 2
N_SHARD = N_Z * N_Y * N_CORE
LINE = N_Y * N_CORE
PIECE = 64
SEQ_LEN = N_SHARD * PIECE
WIDTH = 4096
BLOCK = 512
N_BLOCK = SEQ_LEN // BLOCK
MESH = pl.DeviceIdType.MESH


def kernel(
    proj_ref, bias_ref, cot_ref, context_ref, grad_ref, bias_grad_ref,
    biased, qkv, cot, ctx, grads, dk_acc, dv_acc, ctx_acc, dq_acc, score, dprob, k_t, v_t,
    part, total, stage1, stage2,
    in_send, in_recv, cot_send, cot_recv, out_send, out_recv, ctx_send, ctx_recv,
    s1_send, s1_recv, s2_send, s2_recv,
):
    dp = lax.axis_index("dp")
    section = lax.axis_index("section")
    me = lax.axis_index("shard")
    z, inner = me // LINE, me % LINE
    y, core = inner // N_CORE, inner % N_CORE
    partner = (dp, 1 - section, (N_Z - 1 - z) * LINE + inner)
    scale = HEAD_DIM ** -0.5

    def peer(step):
        to_z = (z + step % N_Z) % N_Z
        rest = step // N_Z
        to_y = (y + rest // N_CORE) % N_Y
        to_core = (core + rest % N_CORE) % N_CORE
        return to_z * LINE + to_y * N_CORE + to_core

    def held_by(shard):
        home = (N_Z - 1 - shard // LINE) * LINE + shard % LINE
        return home // (N_SHARD // 2), (home % (N_SHARD // 2)) * 2

    def same_heads(step):
        return (dp + step // 4) % 4, (section + step // 2 % 2) % 2, ((z // 2 + step % 2) % 2) * 2 + z % 2

    def all_heads(step):
        to_z = z // 2 * 2 + (z % 2 + step // LINE) % 2
        to_y = (y + step % LINE // N_CORE) % N_Y
        to_core = (core + step % N_CORE) % N_CORE
        return to_z * LINE + to_y * N_CORE + to_core

    barrier = pltpu.get_barrier_semaphore()

    def greet_section(step, carry):
        pl.semaphore_signal(barrier, inc=1, device_id=(dp, section, peer(step)), device_id_type=MESH)
        return carry

    lax.fori_loop(1, N_SHARD, greet_section, 0)
    pl.semaphore_signal(barrier, inc=1, device_id=partner, device_id_type=MESH)

    def greet_group(step, carry):
        to_dp, to_section, to_z = same_heads(step)
        pl.semaphore_signal(
            barrier, inc=1, device_id=(to_dp, to_section, to_z * LINE + inner), device_id_type=MESH
        )
        return carry

    lax.fori_loop(2, 16, greet_group, 0)

    for n in range(2):
        for kind in range(3):
            biased[n, kind] = (
                proj_ref[n, kind].astype(jnp.float32) + bias_ref[kind:kind + 1, :]
            ).astype(jnp.bfloat16)

    pl.semaphore_wait(barrier, N_SHARD - 1 + 1 + 14)

    my_seq, my_head = held_by(me)
    my_rows = pl.ds(pl.multiple_of(me * PIECE, PIECE), PIECE)

    def columns(head):
        return pl.ds(pl.multiple_of(head * HEAD_DIM, HEAD_DIM), HEAD_DIM)

    def in_copy(step, h):
        to = peer(step)
        seq, head = held_by(to)
        return pltpu.make_async_remote_copy(
            src_ref=biased.at[seq, :, :, columns(head + h)],
            dst_ref=qkv.at[h, :, my_rows, :],
            send_sem=in_send.at[h, step],
            recv_sem=in_recv.at[h],
            device_id=(dp, section, to),
            device_id_type=MESH,
        )

    def out_copy(step, h):
        to = peer(step)
        rows = pl.ds(pl.multiple_of(to * PIECE, PIECE), PIECE)
        return pltpu.make_async_remote_copy(
            src_ref=grads.at[h, :, rows, :],
            dst_ref=grad_ref.at[my_seq, :, :, columns(my_head + h)],
            send_sem=out_send.at[h, step],
            recv_sem=out_recv,
            device_id=(dp, section, to),
            device_id_type=MESH,
        )

    def cot_copy(h):
        return pltpu.make_async_remote_copy(
            src_ref=cot_ref.at[:, columns(h)],
            dst_ref=cot.at[h],
            send_sem=cot_send.at[h],
            recv_sem=cot_recv.at[h],
            device_id=partner,
            device_id_type=MESH,
        )

    def ctx_copy(h):
        return pltpu.make_async_remote_copy(
            src_ref=ctx.at[h],
            dst_ref=context_ref.at[:, columns(h)],
            send_sem=ctx_send.at[h],
            recv_sem=ctx_recv.at[h],
            device_id=partner,
            device_id_type=MESH,
        )

    def start_in(step, carry):
        in_copy(step, 0).start()
        return carry

    for h in range(2):
        pltpu.make_async_copy(
            biased.at[my_seq, :, :, columns(my_head + h)], qkv.at[h, :, my_rows, :], in_recv.at[h]
        ).start()
    cot_copy(0).start()
    lax.fori_loop(1, N_SHARD, start_in, 0)

    def follow_in(step, carry):
        in_copy(step, 0).wait_send()
        in_copy(step, 1).start()
        return carry

    lax.fori_loop(1, N_SHARD, follow_in, 0)
    cot_copy(1).start()

    part[...] = jnp.zeros_like(part)

    def rows_of(block):
        return pl.ds(pl.multiple_of(block * BLOCK, BLOCK), BLOCK)

    def head_step(h, carry):
        pltpu.make_async_copy(qkv.at[h], qkv.at[h], in_recv.at[h]).wait()

        def turn(c, carry):
            k_t[:, rows_of(c)] = qkv[h, 1, rows_of(c), :].T
            v_t[:, rows_of(c)] = qkv[h, 2, rows_of(c), :].T
            return carry

        lax.fori_loop(0, N_BLOCK, turn, 0)
        dk_acc[...] = jnp.zeros_like(dk_acc)
        dv_acc[...] = jnp.zeros_like(dv_acc)
        cot_copy(h).wait_recv()

        def query_block(b, carry):
            query = qkv[h, 0, rows_of(b), :]
            grad_out = cot[h, rows_of(b), :]
            ctx_acc[...] = jnp.zeros_like(ctx_acc)
            dq_acc[...] = jnp.zeros_like(dq_acc)

            def scores_of(c):
                return lax.dot_general(
                    qkv[h, 1, rows_of(c), :], query, (((1,), (1,)), ((), ())),
                    preferred_element_type=jnp.float32,
                ) * scale

            def first(c, top):
                s = scores_of(c)
                score[rows_of(c), :] = s
                return jnp.maximum(top, jnp.max(s, axis=0, keepdims=True))

            top = lax.fori_loop(0, b, first, jnp.full((1, BLOCK), -jnp.inf, jnp.float32))
            s = scores_of(b)
            key_id = lax.broadcasted_iota(jnp.int32, s.shape, 0)
            query_id = lax.broadcasted_iota(jnp.int32, s.shape, 1)
            s = jnp.where(key_id <= query_id, s, -jnp.inf)
            score[rows_of(b), :] = s
            top = jnp.maximum(top, jnp.max(s, axis=0, keepdims=True))

            def second(c, denom):
                e = jnp.exp(score[rows_of(c), :] - top)
                score[rows_of(c), :] = e
                return denom + jnp.sum(e, axis=0, keepdims=True)

            denom = lax.fori_loop(0, b + 1, second, jnp.zeros((1, BLOCK), jnp.float32))
            inverse = 1.0 / denom

            def third(c, delta):
                probability = score[rows_of(c), :] * inverse
                weights = probability.astype(jnp.bfloat16)
                ctx_acc[...] += jnp.dot(v_t[:, rows_of(c)], weights, preferred_element_type=jnp.float32)
                dv_acc[rows_of(c), :] += jnp.dot(weights, grad_out, preferred_element_type=jnp.float32)
                grad_prob = lax.dot_general(
                    qkv[h, 2, rows_of(c), :], grad_out, (((1,), (1,)), ((), ())),
                    preferred_element_type=jnp.float32,
                )
                dprob[rows_of(c), :] = grad_prob
                return delta + jnp.sum(probability * grad_prob, axis=0, keepdims=True)

            delta = lax.fori_loop(0, b + 1, third, jnp.zeros((1, BLOCK), jnp.float32))

            def fourth(c, carry):
                probability = score[rows_of(c), :] * inverse
                grad_score = (probability * (dprob[rows_of(c), :] - delta) * scale).astype(jnp.bfloat16)
                dq_acc[...] += jnp.dot(k_t[:, rows_of(c)], grad_score, preferred_element_type=jnp.float32)
                dk_acc[rows_of(c), :] += jnp.dot(grad_score, query, preferred_element_type=jnp.float32)
                return carry

            lax.fori_loop(0, b + 1, fourth, 0)
            ctx[h, rows_of(b), :] = ctx_acc[...].T.astype(jnp.bfloat16)
            grads[h, 0, rows_of(b), :] = dq_acc[...].T.astype(jnp.bfloat16)
            return carry

        lax.fori_loop(0, N_BLOCK, query_block, 0)
        ctx_copy(h).start()

        def finish(c, carry):
            dk = dk_acc[rows_of(c), :].astype(jnp.bfloat16)
            dv = dv_acc[rows_of(c), :].astype(jnp.bfloat16)
            grads[h, 1, rows_of(c), :] = dk
            grads[h, 2, rows_of(c), :] = dv
            dq = grads[h, 0, rows_of(c), :]
            return tuple(
                acc + jnp.sum(x.astype(jnp.float32), axis=0, keepdims=True)
                for acc, x in zip(carry, (dq, dk, dv))
            )

        sums = lax.fori_loop(0, N_BLOCK, finish, (jnp.zeros((1, HEAD_DIM), jnp.float32),) * 3)
        for kind in range(3):
            part[h, kind:kind + 1, :] = sums[kind]

        own = pltpu.make_async_copy(
            grads.at[h, :, my_rows, :], grad_ref.at[my_seq, :, :, columns(my_head + h)], out_recv
        )
        own.start()

        def start_out(step, carry):
            out_copy(step, h).start()
            return carry

        lax.fori_loop(1, N_SHARD, start_out, 0)
        return carry

    lax.fori_loop(0, 2, head_step, 0)

    group = (dp * 2 + section) * 2 + z // 2
    pair = my_head // 2

    def s1_copy(step):
        to_dp, to_section, to_z = same_heads(step)
        return pltpu.make_async_remote_copy(
            src_ref=part, dst_ref=stage1.at[group], send_sem=s1_send.at[step], recv_sem=s1_recv,
            device_id=(to_dp, to_section, to_z * LINE + inner), device_id_type=MESH,
        )

    def s2_copy(step):
        return pltpu.make_async_remote_copy(
            src_ref=total, dst_ref=stage2.at[pair], send_sem=s2_send.at[step], recv_sem=s2_recv,
            device_id=(dp, section, all_heads(step)), device_id_type=MESH,
        )

    def run(make, method):
        def body(step, carry):
            getattr(make(step), method)()
            return carry
        lax.fori_loop(1, 16, body, 0)

    pltpu.make_async_copy(part, stage1.at[group], s1_recv).start()
    run(s1_copy, "start")
    pltpu.make_async_copy(stage1, stage1, s1_recv).wait()
    total[...] = jnp.sum(stage1[...], axis=0)
    pltpu.make_async_copy(total, stage2.at[pair], s2_recv).start()
    run(s2_copy, "start")
    pltpu.make_async_copy(stage2, stage2, s2_recv).wait()
    for p in range(16):
        for h in range(2):
            first_column = (p * 2 + h) * HEAD_DIM
            bias_grad_ref[:, first_column:first_column + HEAD_DIM] = stage2[p, h, 0:3, :]
    run(s1_copy, "wait_send")
    run(s2_copy, "wait_send")

    def drain(step, carry):
        in_copy(step, 1).wait_send()
        out_copy(step, 0).wait_send()
        out_copy(step, 1).wait_send()
        return carry

    lax.fori_loop(1, N_SHARD, drain, 0)
    for h in range(2):
        cot_copy(h).wait_send()
        ctx_copy(h).wait_send()
        ctx_copy(h).wait_recv()
    pltpu.make_async_copy(grad_ref, grad_ref, out_recv).wait()


def per_device(projections, bias_terms, context_grad):
    proj = projections[0].transpose(0, 2, 1, 3)
    cot = context_grad.reshape(SEQ_LEN, 2 * HEAD_DIM)
    bf16, f32 = jnp.bfloat16, jnp.float32
    vmem = pl.BlockSpec(memory_space=pltpu.VMEM)
    anywhere = pl.BlockSpec(memory_space=pl.ANY)
    dma = pltpu.SemaphoreType.DMA
    context, grad, bias_grad = pl.pallas_call(
        kernel,
        out_shape=(
            jax.ShapeDtypeStruct((SEQ_LEN, 2 * HEAD_DIM), bf16),
            jax.ShapeDtypeStruct((2, 3, PIECE, WIDTH), bf16),
            jax.ShapeDtypeStruct((3, WIDTH), f32),
        ),
        in_specs=[vmem, vmem, anywhere],
        out_specs=(anywhere, anywhere, vmem),
        scratch_shapes=[
            pltpu.VMEM((2, 3, PIECE, WIDTH), bf16),
            pltpu.VMEM((2, 3, SEQ_LEN, HEAD_DIM), bf16),
            pltpu.VMEM((2, SEQ_LEN, HEAD_DIM), bf16),
            pltpu.VMEM((2, SEQ_LEN, HEAD_DIM), bf16),
            pltpu.VMEM((2, 3, SEQ_LEN, HEAD_DIM), bf16),
            pltpu.VMEM((SEQ_LEN, HEAD_DIM), f32),
            pltpu.VMEM((SEQ_LEN, HEAD_DIM), f32),
            pltpu.VMEM((HEAD_DIM, BLOCK), f32),
            pltpu.VMEM((HEAD_DIM, BLOCK), f32),
            pltpu.VMEM((SEQ_LEN, BLOCK), f32),
            pltpu.VMEM((SEQ_LEN, BLOCK), f32),
            pltpu.VMEM((HEAD_DIM, SEQ_LEN), bf16),
            pltpu.VMEM((HEAD_DIM, SEQ_LEN), bf16),
            pltpu.VMEM((2, 8, HEAD_DIM), f32),
            pltpu.VMEM((2, 8, HEAD_DIM), f32),
            pltpu.VMEM((16, 2, 8, HEAD_DIM), f32),
            pltpu.VMEM((16, 2, 8, HEAD_DIM), f32),
            dma((2, N_SHARD)), dma((2,)),
            dma((2,)), dma((2,)),
            dma((2, N_SHARD)), dma,
            dma((2,)), dma((2,)),
            dma((16,)), dma,
            dma((16,)), dma,
        ],
        compiler_params=pltpu.CompilerParams(
            collective_id=0, has_side_effects=True, vmem_limit_bytes=50 * 2**20
        ),
        cost_estimate=pl.CostEstimate(
            flops=8 * 10**9, bytes_accessed=10 * 2**20, transcendentals=5 * 10**6
        ),
    )(proj, bias_terms, cot)
    return (
        context.reshape(context_grad.shape),
        grad.transpose(0, 2, 1, 3)[None],
        bias_grad,
    )


def solution(mesh):
    placed = (
        P("section", "dp", "shard", None, None),
        P(),
        P("section", "dp", "shard", None, None, None),
    )
    return jax.shard_map(
        per_device,
        mesh=mesh,
        in_specs=placed,
        out_specs=(
            P("section", "dp", "shard", None, None, None),
            P("section", "dp", "shard", None, None),
            P(),
        ),
        check_vma=False,
    )
```

time: 739 us -> 181 us (0.24)
  waiting for transfers between devices: 281 us -> 0 us
  Pallas kernels: 0 us -> 173 us
  blocking collectives: 153 us -> 0 us
  matrix products: 152 us -> 0 us
  local copies, waits for them, and re-layouts: 66.2 us -> 7.56 us
  starting transfers between devices: 53.6 us -> 0 us
  other arithmetic: 24.7 us -> 0 us
    ppermute x2 -> x0, waiting for transfers between devices: 224 us -> none  [partner(): lax.ppermute(x, axis, [(i, i ^ 1 << distance) for i in range(lax.axis_siz...]
    pallas_call x0 -> x1, Pallas kernels: none -> 173 us  [per_device(): pl.pallas_call(kernel, out_shape=(jax.ShapeDtypeStruct((SEQ_LEN, 2 * HEAD...]
    dot_general x22 -> x0, matrix products: 142 us -> none  [the longest x4 52 us: attend_sequence(): jnp.einsum('hqk,khd->qhd', grad_score, key_rows, preferred_element_type=j...]
    all_to_all x1 -> x0, blocking collectives: 77.9 us -> none  [per_device(): lax.all_to_all(for_sending(returning), 'shard', split_axis=0, concat_axis...]
    psum x1 -> x0, blocking collectives: 75.3 us -> none  [per_device(): lax.psum(jnp.sum(seq_grads.astype(jnp.float32), axis=(0, 1)), ('dp', 'sec...]
    all_to_all x1 -> x0, waiting for transfers between devices: 57.8 us -> none  [per_device(): lax.all_to_all(crossed, 'shard', split_axis=0, concat_axis=0, tiled=True)]
    all_to_all x1 -> x0, starting transfers between devices: 42 us -> none  [per_device(): lax.all_to_all(crossed, 'shard', split_axis=0, concat_axis=0, tiled=True)]
    another operation x6 -> x0, local copies, waits for them, and re-layouts: 13.7 us -> none  [the longest x1 5.85 us: per_device(): return (out_context, seq_grads[None], bias_total)]
  transfers between devices with their start and end apart: 3 -> 0, of which waited for: 3 -> 0; matrix products, arithmetic and copies ran while one was open for 4% -> 0% of each run, Pallas kernels for 0% -> 0%
where the time goes in v1:
time: 181 us
  Pallas kernels  173 us (96%)
  local copies, waits for them, and re-layouts  7.56 us (4%)
    pallas_call x1, Pallas kernels, per_device(): pl.pallas_call(kernel, out_shape=(jax.ShapeDtypeStruct((SEQ_LEN, 2 * HEAD...  173 us
    unnamed x7, local copies, waits for them, and re-layouts  7.56 us

profile of v1, /device:TPU:1, one launch (start us, length us, event | category | flops | bytes accessed | tf_op | source)
XLA Modules:
  0.0 180.9 jit_solution(15698838880091264445)
XLA Ops:
  0.6 0.0 copy-start
  0.6 1.2 copy-done
  1.9 0.0 copy-start.1
  1.9 0.8 copy-done.1
  2.7 172.7 %shard_map.58 = (bf16[2048,256]{1,0:T(8,128)(2,1)S(1)}, bf16[2,3,64,4096]{3,2,1,0:T(8,128)(2,1)}, f32[3,4096]{1,0:T(4,128)S(1)}) custom-call(bf16[2,3,64,4096]{3,2,1,0:T(8,128)(2,1)} %bitcast.11, f32[3,4096]{1,0:T(4,128)S(1)} %copy-done.1, bf16[2048,256]{1,0:T(8,128)(2,1)S(1)} %bitcast.9), custom_call_target="tpu_custom_call" | custom-call | flops 8000000000 | bytes 10485760 | tf_op jit(solution)/shard_map/pallas_call | solution.py:318
  175.4 1.0 copy.9
  176.4 3.9 %copy.10 = bf16[1,2,64,3,4096]{4,2,3,1,0:T(8,128)(2,1)} copy(bf16[1,2,64,3,4096]{4,2,3,1,0:T(8,128)(2,1)} %bitcast.10) | data formatting | bytes 6291456
  180.3 0.6 copy.11
Async XLA Ops:
  0.6 1.2 copy-start
  1.9 0.8 copy-start.1

commit v2 on v1

--- a/solution.py
+++ b/solution.py
@@ -15,16 +15,19 @@
 SEQ_LEN = N_SHARD * PIECE
 WIDTH = 4096
 BLOCK = 512
+FIRST_OUT = 24
+CHUNK = 512
+N_CHUNK = SEQ_LEN // CHUNK
 N_BLOCK = SEQ_LEN // BLOCK
 MESH = pl.DeviceIdType.MESH
 
 
 def kernel(
-    proj_ref, bias_ref, cot_ref, context_ref, grad_ref, bias_grad_ref,
-    biased, qkv, cot, ctx, grads, dk_acc, dv_acc, ctx_acc, dq_acc, score, dprob, k_t, v_t,
+    proj_ref, bias_hbm, cot_ref, context_ref, grad_ref, bias_grad_ref,
+    biased, bias_ref, qkv, cot, ctx, grads, dk_acc, dv_acc, ctx_acc, dq_acc, score, dprob, k_t, v_t,
     part, total, stage1, stage2,
     in_send, in_recv, cot_send, cot_recv, out_send, out_recv, ctx_send, ctx_recv,
-    s1_send, s1_recv, s2_send, s2_recv,
+    s1_send, s1_recv, s2_send, s2_recv, load_sem, bias_sem,
 ):
     dp = lax.axis_index("dp")
     section = lax.axis_index("section")
@@ -54,6 +57,15 @@
         to_core = (core + step % N_CORE) % N_CORE
         return to_z * LINE + to_y * N_CORE + to_core
 
+    def load(n, kind):
+        return pltpu.make_async_copy(proj_ref.at[n, kind], biased.at[n, kind], load_sem.at[n, kind])
+
+    load_bias = pltpu.make_async_copy(bias_hbm, bias_ref, bias_sem)
+    load_bias.start()
+    for n in range(2):
+        for kind in range(3):
+            load(n, kind).start()
+
     barrier = pltpu.get_barrier_semaphore()
 
     def greet_section(step, carry):
@@ -72,10 +84,12 @@
 
     lax.fori_loop(2, 16, greet_group, 0)
 
+    load_bias.wait()
     for n in range(2):
         for kind in range(3):
+            load(n, kind).wait()
             biased[n, kind] = (
-                proj_ref[n, kind].astype(jnp.float32) + bias_ref[kind:kind + 1, :]
+                biased[n, kind].astype(jnp.float32) + bias_ref[kind:kind + 1, :]
             ).astype(jnp.bfloat16)
 
     pl.semaphore_wait(barrier, N_SHARD - 1 + 1 + 14)
@@ -110,25 +124,34 @@
             device_id_type=MESH,
         )
 
-    def cot_copy(h):
-        return pltpu.make_async_remote_copy(
-            src_ref=cot_ref.at[:, columns(h)],
-            dst_ref=cot.at[h],
-            send_sem=cot_send.at[h],
+    def chunk_rows(chunk):
+        return pl.ds(pl.multiple_of(chunk * CHUNK, CHUNK), CHUNK)
+
+    def cot_copy(h, chunk):
+        return pltpu.make_async_remote_copy(
+            src_ref=cot_ref.at[chunk_rows(chunk), columns(h)],
+            dst_ref=cot.at[h, chunk_rows(chunk), :],
+            send_sem=cot_send.at[h, chunk],
             recv_sem=cot_recv.at[h],
             device_id=partner,
             device_id_type=MESH,
         )
 
-    def ctx_copy(h):
-        return pltpu.make_async_remote_copy(
-            src_ref=ctx.at[h],
-            dst_ref=context_ref.at[:, columns(h)],
-            send_sem=ctx_send.at[h],
-            recv_sem=ctx_recv.at[h],
+    def ctx_copy(h, chunk):
+        return pltpu.make_async_remote_copy(
+            src_ref=ctx.at[h, chunk_rows(chunk), :],
+            dst_ref=context_ref.at[chunk_rows(chunk), columns(h)],
+            send_sem=ctx_send.at[h, chunk],
+            recv_sem=ctx_recv,
             device_id=partner,
             device_id_type=MESH,
         )
+
+    def start_cot(h):
+        def body(chunk, carry):
+            cot_copy(h, chunk).start()
+            return carry
+        lax.fori_loop(0, N_CHUNK, body, 0)
 
     def start_in(step, carry):
         in_copy(step, 0).start()
@@ -138,7 +161,7 @@
         pltpu.make_async_copy(
             biased.at[my_seq, :, :, columns(my_head + h)], qkv.at[h, :, my_rows, :], in_recv.at[h]
         ).start()
-    cot_copy(0).start()
+    start_cot(0)
     lax.fori_loop(1, N_SHARD, start_in, 0)
 
     def follow_in(step, carry):
@@ -147,12 +170,34 @@
         return carry
 
     lax.fori_loop(1, N_SHARD, follow_in, 0)
-    cot_copy(1).start()
+    start_cot(1)
 
     part[...] = jnp.zeros_like(part)
 
     def rows_of(block):
         return pl.ds(pl.multiple_of(block * BLOCK, BLOCK), BLOCK)
+
+    group = (dp * 2 + section) * 2 + z // 2
+    pair = my_head // 2
+
+    def s1_copy(step):
+        to_dp, to_section, to_z = same_heads(step)
+        return pltpu.make_async_remote_copy(
+            src_ref=part, dst_ref=stage1.at[group], send_sem=s1_send.at[step], recv_sem=s1_recv,
+            device_id=(to_dp, to_section, to_z * LINE + inner), device_id_type=MESH,
+        )
+
+    def s2_copy(step):
+        return pltpu.make_async_remote_copy(
+            src_ref=total, dst_ref=stage2.at[pair], send_sem=s2_send.at[step], recv_sem=s2_recv,
+            device_id=(dp, section, all_heads(step)), device_id_type=MESH,
+        )
+
+    def run(make, method):
+        def body(step, carry):
+            getattr(make(step), method)()
+            return carry
+        lax.fori_loop(1, 16, body, 0)
 
     def head_step(h, carry):
         pltpu.make_async_copy(qkv.at[h], qkv.at[h], in_recv.at[h]).wait()
@@ -165,7 +210,7 @@
         lax.fori_loop(0, N_BLOCK, turn, 0)
         dk_acc[...] = jnp.zeros_like(dk_acc)
         dv_acc[...] = jnp.zeros_like(dv_acc)
-        cot_copy(h).wait_recv()
+        pltpu.make_async_copy(cot.at[h], cot.at[h], cot_recv.at[h]).wait()
 
         def query_block(b, carry):
             query = qkv[h, 0, rows_of(b), :]
@@ -224,10 +269,11 @@
             lax.fori_loop(0, b + 1, fourth, 0)
             ctx[h, rows_of(b), :] = ctx_acc[...].T.astype(jnp.bfloat16)
             grads[h, 0, rows_of(b), :] = dq_acc[...].T.astype(jnp.bfloat16)
+            for part_id in range(BLOCK // CHUNK):
+                ctx_copy(h, b * (BLOCK // CHUNK) + part_id).start()
             return carry
 
         lax.fori_loop(0, N_BLOCK, query_block, 0)
-        ctx_copy(h).start()
 
         def finish(c, carry):
             dk = dk_acc[rows_of(c), :].astype(jnp.bfloat16)
@@ -242,7 +288,12 @@
 
         sums = lax.fori_loop(0, N_BLOCK, finish, (jnp.zeros((1, HEAD_DIM), jnp.float32),) * 3)
         for kind in range(3):
-            part[h, kind:kind + 1, :] = sums[kind]
+            part[pl.ds(h * 3 + kind, 1), :] = sums[kind]
+
+        @pl.when(h == 1)
+        def _():
+            pltpu.make_async_copy(part, stage1.at[group], s1_recv).start()
+            run(s1_copy, "start")
 
         own = pltpu.make_async_copy(
             grads.at[h, :, my_rows, :], grad_ref.at[my_seq, :, :, columns(my_head + h)], out_recv
@@ -253,44 +304,25 @@
             out_copy(step, h).start()
             return carry
 
-        lax.fori_loop(1, N_SHARD, start_out, 0)
+        lax.fori_loop(1, FIRST_OUT, start_out, 0)
+
+        @pl.when(h == 1)
+        def _():
+            pltpu.make_async_copy(stage1, stage1, s1_recv).wait()
+            total[...] = jnp.sum(stage1[...], axis=0)
+            pltpu.make_async_copy(total, stage2.at[pair], s2_recv).start()
+            run(s2_copy, "start")
+
+        lax.fori_loop(FIRST_OUT, N_SHARD, start_out, 0)
         return carry
 
     lax.fori_loop(0, 2, head_step, 0)
 
-    group = (dp * 2 + section) * 2 + z // 2
-    pair = my_head // 2
-
-    def s1_copy(step):
-        to_dp, to_section, to_z = same_heads(step)
-        return pltpu.make_async_remote_copy(
-            src_ref=part, dst_ref=stage1.at[group], send_sem=s1_send.at[step], recv_sem=s1_recv,
-            device_id=(to_dp, to_section, to_z * LINE + inner), device_id_type=MESH,
-        )
-
-    def s2_copy(step):
-        return pltpu.make_async_remote_copy(
-            src_ref=total, dst_ref=stage2.at[pair], send_sem=s2_send.at[step], recv_sem=s2_recv,
-            device_id=(dp, section, all_heads(step)), device_id_type=MESH,
-        )
-
-    def run(make, method):
-        def body(step, carry):
-            getattr(make(step), method)()
-            return carry
-        lax.fori_loop(1, 16, body, 0)
-
-    pltpu.make_async_copy(part, stage1.at[group], s1_recv).start()
-    run(s1_copy, "start")
-    pltpu.make_async_copy(stage1, stage1, s1_recv).wait()
-    total[...] = jnp.sum(stage1[...], axis=0)
-    pltpu.make_async_copy(total, stage2.at[pair], s2_recv).start()
-    run(s2_copy, "start")
     pltpu.make_async_copy(stage2, stage2, s2_recv).wait()
     for p in range(16):
         for h in range(2):
             first_column = (p * 2 + h) * HEAD_DIM
-            bias_grad_ref[:, first_column:first_column + HEAD_DIM] = stage2[p, h, 0:3, :]
+            bias_grad_ref[:, first_column:first_column + HEAD_DIM] = stage2[p, h * 3:h * 3 + 3, :]
     run(s1_copy, "wait_send")
     run(s2_copy, "wait_send")
 
@@ -301,10 +333,15 @@
         return carry
 
     lax.fori_loop(1, N_SHARD, drain, 0)
-    for h in range(2):
-        cot_copy(h).wait_send()
-        ctx_copy(h).wait_send()
-        ctx_copy(h).wait_recv()
+
+    def drain_chunks(chunk, carry):
+        for h in range(2):
+            cot_copy(h, chunk).wait_send()
+            ctx_copy(h, chunk).wait_send()
+        return carry
+
+    lax.fori_loop(0, N_CHUNK, drain_chunks, 0)
+    pltpu.make_async_copy(context_ref, context_ref, ctx_recv).wait()
     pltpu.make_async_copy(grad_ref, grad_ref, out_recv).wait()
 
 
@@ -314,6 +351,7 @@
     bf16, f32 = jnp.bfloat16, jnp.float32
     vmem = pl.BlockSpec(memory_space=pltpu.VMEM)
     anywhere = pl.BlockSpec(memory_space=pl.ANY)
+    hbm = pl.BlockSpec(memory_space=pltpu.HBM)
     dma = pltpu.SemaphoreType.DMA
     context, grad, bias_grad = pl.pallas_call(
         kernel,
@@ -322,10 +360,11 @@
             jax.ShapeDtypeStruct((2, 3, PIECE, WIDTH), bf16),
             jax.ShapeDtypeStruct((3, WIDTH), f32),
         ),
-        in_specs=[vmem, vmem, anywhere],
+        in_specs=[hbm, hbm, hbm],
         out_specs=(anywhere, anywhere, vmem),
         scratch_shapes=[
             pltpu.VMEM((2, 3, PIECE, WIDTH), bf16),
+            pltpu.VMEM((3, WIDTH), f32),
             pltpu.VMEM((2, 3, SEQ_LEN, HEAD_DIM), bf16),
             pltpu.VMEM((2, SEQ_LEN, HEAD_DIM), bf16),
             pltpu.VMEM((2, SEQ_LEN, HEAD_DIM), bf16),
@@ -338,24 +377,25 @@
             pltpu.VMEM((SEQ_LEN, BLOCK), f32),
             pltpu.VMEM((HEAD_DIM, SEQ_LEN), bf16),
             pltpu.VMEM((HEAD_DIM, SEQ_LEN), bf16),
-            pltpu.VMEM((2, 8, HEAD_DIM), f32),
-            pltpu.VMEM((2, 8, HEAD_DIM), f32),
-            pltpu.VMEM((16, 2, 8, HEAD_DIM), f32),
-            pltpu.VMEM((16, 2, 8, HEAD_DIM), f32),
+            pltpu.VMEM((8, HEAD_DIM), f32),
+            pltpu.VMEM((8, HEAD_DIM), f32),
+            pltpu.VMEM((16, 8, HEAD_DIM), f32),
+            pltpu.VMEM((16, 8, HEAD_DIM), f32),
             dma((2, N_SHARD)), dma((2,)),
-            dma((2,)), dma((2,)),
+            dma((2, N_CHUNK)), dma((2,)),
             dma((2, N_SHARD)), dma,
-            dma((2,)), dma((2,)),
+            dma((2, N_CHUNK)), dma,
             dma((16,)), dma,
             dma((16,)), dma,
+            dma((2, 3)), dma,
         ],
         compiler_params=pltpu.CompilerParams(
-            collective_id=0, has_side_effects=True, vmem_limit_bytes=50 * 2**20
+            collective_id=0, has_side_effects=True, vmem_limit_bytes=36 * 2**20
         ),
         cost_estimate=pl.CostEstimate(
             flops=8 * 10**9, bytes_accessed=10 * 2**20, transcendentals=5 * 10**6
         ),
-    )(proj, bias_terms, cot)
+    )(*(pltpu.with_memory_space_constraint(x, pltpu.HBM) for x in (proj, bias_terms, cot)))
     return (
         context.reshape(context_grad.shape),
         grad.transpose(0, 2, 1, 3)[None],

time: 181 us -> 169 us (0.934)
  Pallas kernels: 173 us -> 165 us
  local copies, waits for them, and re-layouts: 7.56 us -> 3.27 us
    pallas_call x1, Pallas kernels: 173 us -> 165 us  [per_device(): pl.pallas_call(kernel, out_shape=(jax.ShapeDtypeStruct((SEQ_LEN, 2 * HEAD...]
    unnamed x7 -> x3, local copies, waits for them, and re-layouts: 7.56 us -> 3.27 us
where the time goes in v2:
time: 169 us; the launch traced here: 168 us
  Pallas kernels  165 us (98%)
  local copies, waits for them, and re-layouts  3.27 us (2%)
    pallas_call x1, Pallas kernels, per_device(): pl.pallas_call(kernel, out_shape=(jax.ShapeDtypeStruct((SEQ_LEN, 2 * HEAD...  165 us

profile of v2, /device:TPU:1, one launch (start us, length us, event | category | flops | bytes accessed | tf_op | source)
XLA Modules:
  0.0 168.5 jit_solution(8314304749435822226)
XLA Ops:
  0.6 164.6 %shard_map.58 = (bf16[2048,256]{1,0:T(8,128)(2,1)S(1)}, bf16[2,3,64,4096]{3,2,1,0:T(8,128)(2,1)S(1)}, f32[3,4096]{1,0:T(4,128)S(1)}) custom-call(bf16[2,3,64,4096]{3,2,1,0:T(8,128)(2,1)} %bitcast.10, f32[3,4096]{1,0:T(4,128)} %bias_hbm.1, bf16[2048,256]{1,0:T(8,128)(2,1)} %bitcast.11), custom_call_target="tpu_custom_call" | custom-call | flops 8000000000 | bytes 10485760 | tf_op jit(solution)/shard_map/pallas_call | solution.py:356
  165.2 1.0 copy.9
  166.2 1.7 copy.10
  167.8 0.6 copy.11

commit v3 on v2

--- a/solution.py
+++ b/solution.py
@@ -15,7 +15,7 @@
 SEQ_LEN = N_SHARD * PIECE
 WIDTH = 4096
 BLOCK = 512
-FIRST_OUT = 24
+FIRST_OUT = 28
 CHUNK = 512
 N_CHUNK = SEQ_LEN // CHUNK
 N_BLOCK = SEQ_LEN // BLOCK
@@ -27,35 +27,73 @@
     biased, bias_ref, qkv, cot, ctx, grads, dk_acc, dv_acc, ctx_acc, dq_acc, score, dprob, k_t, v_t,
     part, total, stage1, stage2,
     in_send, in_recv, cot_send, cot_recv, out_send, out_recv, ctx_send, ctx_recv,
-    s1_send, s1_recv, s2_send, s2_recv, load_sem, bias_sem,
+    s1_send, s1_recv, s2_send, s2_recv, load_sem, bias_sem, ready,
 ):
     dp = lax.axis_index("dp")
     section = lax.axis_index("section")
     me = lax.axis_index("shard")
-    z, inner = me // LINE, me % LINE
-    y, core = inner // N_CORE, inner % N_CORE
+    z, inner = lax.div(me, LINE), lax.rem(me, LINE)
+    y, core = lax.div(inner, N_CORE), lax.rem(inner, N_CORE)
     partner = (dp, 1 - section, (N_Z - 1 - z) * LINE + inner)
     scale = HEAD_DIM ** -0.5
 
+    def split(value, by):
+        if isinstance(value, int):
+            return value // by, value % by
+        return lax.div(value, by), lax.rem(value, by)
+
     def peer(step):
-        to_z = (z + step % N_Z) % N_Z
-        rest = step // N_Z
-        to_y = (y + rest // N_CORE) % N_Y
-        to_core = (core + rest % N_CORE) % N_CORE
+        rest, step_z = split(step, N_Z)
+        step_y, step_core = split(rest, N_CORE)
+        to_z = lax.rem(z + step_z, N_Z)
+        to_y = lax.rem(y + step_y, N_Y)
+        to_core = lax.rem(core + step_core, N_CORE)
         return to_z * LINE + to_y * N_CORE + to_core
 
     def held_by(shard):
-        home = (N_Z - 1 - shard // LINE) * LINE + shard % LINE
-        return home // (N_SHARD // 2), (home % (N_SHARD // 2)) * 2
+        shard_z, shard_inner = split(shard, LINE)
+        home_z = N_Z - 1 - shard_z
+        seq, odd = split(home_z, 2)
+        return seq, (odd * LINE + shard_inner) * 2
+
+    z_pair, z_odd = split(z, 2)
 
     def same_heads(step):
-        return (dp + step // 4) % 4, (section + step // 2 % 2) % 2, ((z // 2 + step % 2) % 2) * 2 + z % 2
+        rest, step_pair = split(step, 2)
+        step_dp, step_section = split(rest, 2)
+        to_pair = lax.rem(z_pair + step_pair, 2)
+        return lax.rem(dp + step_dp, 4), lax.rem(section + step_section, 2), to_pair * 2 + z_odd
 
     def all_heads(step):
-        to_z = z // 2 * 2 + (z % 2 + step // LINE) % 2
-        to_y = (y + step % LINE // N_CORE) % N_Y
-        to_core = (core + step % N_CORE) % N_CORE
+        step_odd, rest = split(step, LINE)
+        step_y, step_core = split(rest, N_CORE)
+        to_z = z_pair * 2 + lax.rem(z_odd + step_odd, 2)
+        to_y = lax.rem(y + step_y, N_Y)
+        to_core = lax.rem(core + step_core, N_CORE)
         return to_z * LINE + to_y * N_CORE + to_core
+
+    barrier = pltpu.get_barrier_semaphore()
+
+    def tell(sem, device):
+        pl.semaphore_signal(sem, inc=1, device_id=device, device_id_type=MESH)
+
+    def group_device(step):
+        to_dp, to_section, to_z = same_heads(step)
+        return to_dp, to_section, to_z * LINE + inner
+
+    near = [step for step in range(2, 16) if step // 2 % 2 == 0]
+    far = [step for step in range(2, 16) if step // 2 % 2 == 1]
+
+    for step in range(1, N_SHARD):
+        tell(barrier, (dp, section, peer(step)))
+    for step in near:
+        tell(barrier, group_device(step))
+
+    @pl.when(section == 0)
+    def _():
+        tell(barrier, partner)
+        for step in far:
+            tell(barrier, group_device(step))
 
     def load(n, kind):
         return pltpu.make_async_copy(proj_ref.at[n, kind], biased.at[n, kind], load_sem.at[n, kind])
@@ -65,24 +103,6 @@
     for n in range(2):
         for kind in range(3):
             load(n, kind).start()
-
-    barrier = pltpu.get_barrier_semaphore()
-
-    def greet_section(step, carry):
-        pl.semaphore_signal(barrier, inc=1, device_id=(dp, section, peer(step)), device_id_type=MESH)
-        return carry
-
-    lax.fori_loop(1, N_SHARD, greet_section, 0)
-    pl.semaphore_signal(barrier, inc=1, device_id=partner, device_id_type=MESH)
-
-    def greet_group(step, carry):
-        to_dp, to_section, to_z = same_heads(step)
-        pl.semaphore_signal(
-            barrier, inc=1, device_id=(to_dp, to_section, to_z * LINE + inner), device_id_type=MESH
-        )
-        return carry
-
-    lax.fori_loop(2, 16, greet_group, 0)
 
     load_bias.wait()
     for n in range(2):
@@ -92,7 +112,16 @@
                 biased[n, kind].astype(jnp.float32) + bias_ref[kind:kind + 1, :]
             ).astype(jnp.bfloat16)
 
-    pl.semaphore_wait(barrier, N_SHARD - 1 + 1 + 14)
+    @pl.when(section == 0)
+    def _():
+        pl.semaphore_wait(barrier, N_SHARD - 1 + len(near))
+
+    @pl.when(section == 1)
+    def _():
+        pl.semaphore_wait(barrier, N_SHARD - 1 + len(near) + 1 + len(far))
+        tell(ready, partner)
+        for step in far:
+            tell(ready, group_device(step))
 
     my_seq, my_head = held_by(me)
     my_rows = pl.ds(pl.multiple_of(me * PIECE, PIECE), PIECE)
@@ -161,8 +190,13 @@
         pltpu.make_async_copy(
             biased.at[my_seq, :, :, columns(my_head + h)], qkv.at[h, :, my_rows, :], in_recv.at[h]
         ).start()
+    lax.fori_loop(1, N_SHARD, start_in, 0)
+
+    @pl.when(section == 0)
+    def _():
+        pl.semaphore_wait(ready, 1 + len(far))
+
     start_cot(0)
-    lax.fori_loop(1, N_SHARD, start_in, 0)
 
     def follow_in(step, carry):
         in_copy(step, 0).wait_send()
@@ -177,8 +211,8 @@
     def rows_of(block):
         return pl.ds(pl.multiple_of(block * BLOCK, BLOCK), BLOCK)
 
-    group = (dp * 2 + section) * 2 + z // 2
-    pair = my_head // 2
+    group = (dp * 2 + section) * 2 + z_pair
+    pair = lax.div(my_head, 2)
 
     def s1_copy(step):
         to_dp, to_section, to_z = same_heads(step)
@@ -388,6 +422,7 @@
             dma((16,)), dma,
             dma((16,)), dma,
             dma((2, 3)), dma,
+            pltpu.SemaphoreType.REGULAR,
         ],
         compiler_params=pltpu.CompilerParams(
             collective_id=0, has_side_effects=True, vmem_limit_bytes=36 * 2**20

time: 169 us -> 165 us (0.976)
  Pallas kernels: 165 us -> 161 us
    pallas_call x1, Pallas kernels: 165 us -> 161 us  [per_device(): pl.pallas_call(kernel, out_shape=(jax.ShapeDtypeStruct((SEQ_LEN, 2 * HEAD...]
where the time goes in v3:
time: 165 us
  Pallas kernels  161 us (98%)
  local copies, waits for them, and re-layouts  3.27 us (2%)
    pallas_call x1, Pallas kernels, per_device(): pl.pallas_call(kernel, out_shape=(jax.ShapeDtypeStruct((SEQ_LEN, 2 * HEAD...  161 us

profile of v3, /device:TPU:1, one launch (start us, length us, event | category | flops | bytes accessed | tf_op | source)
XLA Modules:
  0.0 165.2 jit_solution(13989281142965378618)
XLA Ops:
  0.6 161.3 %shard_map.58 = (bf16[2048,256]{1,0:T(8,128)(2,1)S(1)}, bf16[2,3,64,4096]{3,2,1,0:T(8,128)(2,1)S(1)}, f32[3,4096]{1,0:T(4,128)S(1)}) custom-call(bf16[2,3,64,4096]{3,2,1,0:T(8,128)(2,1)} %bitcast.10, f32[3,4096]{1,0:T(4,128)} %bias_hbm.1, bf16[2048,256]{1,0:T(8,128)(2,1)} %bitcast.11), custom_call_target="tpu_custom_call" | custom-call | flops 8000000000 | bytes 10485760 | tf_op jit(solution)/shard_map/pallas_call | solution.py:390
  161.9 1.0 copy.9
  162.9 1.7 %copy.10 = bf16[1,2,64,3,4096]{4,2,3,1,0:T(8,128)(2,1)} copy(bf16[1,2,64,3,4096]{4,2,3,1,0:T(8,128)(2,1)S(1)} %bitcast.8) | data formatting | bytes 6291456
  164.6 0.6 copy.11

commit v4 on v3

--- a/solution.py
+++ b/solution.py
@@ -8,14 +8,15 @@
 from jax.sharding import PartitionSpec as P
 
 HEAD_DIM = 128
-N_Z, N_Y, N_CORE = 4, 4, 2
+N_DP, N_Z, N_Y, N_CORE = 4, 4, 4, 2
 N_SHARD = N_Z * N_Y * N_CORE
 LINE = N_Y * N_CORE
 PIECE = 64
 SEQ_LEN = N_SHARD * PIECE
 WIDTH = 4096
 BLOCK = 512
-FIRST_OUT = 28
+SECOND_STAGE = 16
+THIRD_STAGE = 26
 CHUNK = 512
 N_CHUNK = SEQ_LEN // CHUNK
 N_BLOCK = SEQ_LEN // BLOCK
@@ -25,9 +26,9 @@
 def kernel(
     proj_ref, bias_hbm, cot_ref, context_ref, grad_ref, bias_grad_ref,
     biased, bias_ref, qkv, cot, ctx, grads, dk_acc, dv_acc, ctx_acc, dq_acc, score, dprob, k_t, v_t,
-    part, total, stage1, stage2,
+    part, total, pairs, stage1, stage2, stage3,
     in_send, in_recv, cot_send, cot_recv, out_send, out_recv, ctx_send, ctx_recv,
-    s1_send, s1_recv, s2_send, s2_recv, load_sem, bias_sem, ready,
+    s1_send, s1_recv, s2_send, s2_recv, s3_send, s3_recv, load_sem, bias_sem, ready,
 ):
     dp = lax.axis_index("dp")
     section = lax.axis_index("section")
@@ -43,7 +44,7 @@
         return lax.div(value, by), lax.rem(value, by)
 
     def peer(step):
-        rest, step_z = split(step, N_Z)
+        rest, step_z = split(N_SHARD - step, N_Z)
         step_y, step_core = split(rest, N_CORE)
         to_z = lax.rem(z + step_z, N_Z)
         to_y = lax.rem(y + step_y, N_Y)
@@ -56,44 +57,38 @@
         seq, odd = split(home_z, 2)
         return seq, (odd * LINE + shard_inner) * 2
 
-    z_pair, z_odd = split(z, 2)
-
-    def same_heads(step):
-        rest, step_pair = split(step, 2)
-        step_dp, step_section = split(rest, 2)
-        to_pair = lax.rem(z_pair + step_pair, 2)
-        return lax.rem(dp + step_dp, 4), lax.rem(section + step_section, 2), to_pair * 2 + z_odd
-
-    def all_heads(step):
-        step_odd, rest = split(step, LINE)
-        step_y, step_core = split(rest, N_CORE)
-        to_z = z_pair * 2 + lax.rem(z_odd + step_odd, 2)
+    ring = section * N_Z + z
+
+    def dp_device(step):
+        return lax.rem(dp + step, N_DP), section, me
+
+    def ring_device(step):
+        to_section, to_z = split(lax.rem(ring + step, 2 * N_Z), N_Z)
+        return dp, to_section, to_z * LINE + inner
+
+    def plane_device(step):
+        step_y, step_core = split(step, N_CORE)
         to_y = lax.rem(y + step_y, N_Y)
         to_core = lax.rem(core + step_core, N_CORE)
-        return to_z * LINE + to_y * N_CORE + to_core
+        return dp, section, z * LINE + to_y * N_CORE + to_core
 
     barrier = pltpu.get_barrier_semaphore()
 
     def tell(sem, device):
         pl.semaphore_signal(sem, inc=1, device_id=device, device_id_type=MESH)
 
-    def group_device(step):
-        to_dp, to_section, to_z = same_heads(step)
-        return to_dp, to_section, to_z * LINE + inner
-
-    near = [step for step in range(2, 16) if step // 2 % 2 == 0]
-    far = [step for step in range(2, 16) if step // 2 % 2 == 1]
+    def other_section(h):
+        return dp, 1 - section, h * LINE + inner
 
     for step in range(1, N_SHARD):
         tell(barrier, (dp, section, peer(step)))
-    for step in near:
-        tell(barrier, group_device(step))
+    for step in range(1, N_DP):
+        tell(barrier, dp_device(step))
 
     @pl.when(section == 0)
     def _():
-        tell(barrier, partner)
-        for step in far:
-            tell(barrier, group_device(step))
+        for far_z in range(N_Z):
+            tell(barrier, other_section(far_z))
 
     def load(n, kind):
         return pltpu.make_async_copy(proj_ref.at[n, kind], biased.at[n, kind], load_sem.at[n, kind])
@@ -114,14 +109,13 @@
 
     @pl.when(section == 0)
     def _():
-        pl.semaphore_wait(barrier, N_SHARD - 1 + len(near))
+        pl.semaphore_wait(barrier, N_SHARD - 1 + N_DP - 1)
 
     @pl.when(section == 1)
     def _():
-        pl.semaphore_wait(barrier, N_SHARD - 1 + len(near) + 1 + len(far))
-        tell(ready, partner)
-        for step in far:
-            tell(ready, group_device(step))
+        pl.semaphore_wait(barrier, N_SHARD - 1 + N_DP - 1 + N_Z)
+        for far_z in range(N_Z):
+            tell(ready, other_section(far_z))
 
     my_seq, my_head = held_by(me)
     my_rows = pl.ds(pl.multiple_of(me * PIECE, PIECE), PIECE)
@@ -194,7 +188,7 @@
 
     @pl.when(section == 0)
     def _():
-        pl.semaphore_wait(ready, 1 + len(far))
+        pl.semaphore_wait(ready, N_Z)
 
     start_cot(0)
 
@@ -211,27 +205,33 @@
     def rows_of(block):
         return pl.ds(pl.multiple_of(block * BLOCK, BLOCK), BLOCK)
 
-    group = (dp * 2 + section) * 2 + z_pair
-    pair = lax.div(my_head, 2)
+    def stage_copy(src, dst, sends, recv, device):
+        return pltpu.make_async_remote_copy(
+            src_ref=src, dst_ref=dst, send_sem=sends, recv_sem=recv, device_id=device, device_id_type=MESH
+        )
 
     def s1_copy(step):
-        to_dp, to_section, to_z = same_heads(step)
-        return pltpu.make_async_remote_copy(
-            src_ref=part, dst_ref=stage1.at[group], send_sem=s1_send.at[step], recv_sem=s1_recv,
-            device_id=(to_dp, to_section, to_z * LINE + inner), device_id_type=MESH,
-        )
+        return stage_copy(part, stage1.at[dp], s1_send.at[step], s1_recv, dp_device(step))
 
     def s2_copy(step):
-        return pltpu.make_async_remote_copy(
-            src_ref=total, dst_ref=stage2.at[pair], send_sem=s2_send.at[step], recv_sem=s2_recv,
-            device_id=(dp, section, all_heads(step)), device_id_type=MESH,
-        )
-
-    def run(make, method):
+        return stage_copy(total, stage2.at[ring], s2_send.at[step], s2_recv, ring_device(step))
+
+    def s3_copy(step):
+        return stage_copy(pairs, stage3.at[inner], s3_send.at[step], s3_recv, plane_device(step))
+
+    def begin(make, src, dst, recv, count):
+        pltpu.make_async_copy(src, dst, recv).start()
+
         def body(step, carry):
-            getattr(make(step), method)()
-            return carry
-        lax.fori_loop(1, 16, body, 0)
+            make(step).start()
+            return carry
+        lax.fori_loop(1, count, body, 0)
+
+    def sent(make, count):
+        def body(step, carry):
+            make(step).wait_send()
+            return carry
+        lax.fori_loop(1, count, body, 0)
 
     def head_step(h, carry):
         pltpu.make_async_copy(qkv.at[h], qkv.at[h], in_recv.at[h]).wait()
@@ -326,8 +326,7 @@
 
         @pl.when(h == 1)
         def _():
-            pltpu.make_async_copy(part, stage1.at[group], s1_recv).start()
-            run(s1_copy, "start")
+            begin(s1_copy, part, stage1.at[dp], s1_recv, N_DP)
 
         own = pltpu.make_async_copy(
             grads.at[h, :, my_rows, :], grad_ref.at[my_seq, :, :, columns(my_head + h)], out_recv
@@ -338,27 +337,37 @@
             out_copy(step, h).start()
             return carry
 
-        lax.fori_loop(1, FIRST_OUT, start_out, 0)
+        lax.fori_loop(1, SECOND_STAGE, start_out, 0)
 
         @pl.when(h == 1)
         def _():
             pltpu.make_async_copy(stage1, stage1, s1_recv).wait()
             total[...] = jnp.sum(stage1[...], axis=0)
-            pltpu.make_async_copy(total, stage2.at[pair], s2_recv).start()
-            run(s2_copy, "start")
-
-        lax.fori_loop(FIRST_OUT, N_SHARD, start_out, 0)
+            begin(s2_copy, total, stage2.at[ring], s2_recv, 2 * N_Z)
+
+        lax.fori_loop(SECOND_STAGE, THIRD_STAGE, start_out, 0)
+
+        @pl.when(h == 1)
+        def _():
+            pltpu.make_async_copy(stage2, stage2, s2_recv).wait()
+            for odd in range(2):
+                pairs[odd] = stage2[1 - odd] + stage2[3 - odd] + stage2[5 - odd] + stage2[7 - odd]
+            begin(s3_copy, pairs, stage3.at[inner], s3_recv, LINE)
+
+        lax.fori_loop(THIRD_STAGE, N_SHARD, start_out, 0)
         return carry
 
     lax.fori_loop(0, 2, head_step, 0)
 
-    pltpu.make_async_copy(stage2, stage2, s2_recv).wait()
-    for p in range(16):
-        for h in range(2):
-            first_column = (p * 2 + h) * HEAD_DIM
-            bias_grad_ref[:, first_column:first_column + HEAD_DIM] = stage2[p, h * 3:h * 3 + 3, :]
-    run(s1_copy, "wait_send")
-    run(s2_copy, "wait_send")
+    pltpu.make_async_copy(stage3, stage3, s3_recv).wait()
+    for odd in range(2):
+        for p in range(LINE):
+            for h in range(2):
+                first_column = ((odd * LINE + p) * 2 + h) * HEAD_DIM
+                bias_grad_ref[:, first_column:first_column + HEAD_DIM] = stage3[p, odd, h * 3:h * 3 + 3, :]
+    sent(s1_copy, N_DP)
+    sent(s2_copy, 2 * N_Z)
+    sent(s3_copy, LINE)
 
     def drain(step, carry):
         in_copy(step, 1).wait_send()
@@ -413,14 +422,17 @@
             pltpu.VMEM((HEAD_DIM, SEQ_LEN), bf16),
             pltpu.VMEM((8, HEAD_DIM), f32),
             pltpu.VMEM((8, HEAD_DIM), f32),
-            pltpu.VMEM((16, 8, HEAD_DIM), f32),
-            pltpu.VMEM((16, 8, HEAD_DIM), f32),
+            pltpu.VMEM((2, 8, HEAD_DIM), f32),
+            pltpu.VMEM((N_DP, 8, HEAD_DIM), f32),
+            pltpu.VMEM((2 * N_Z, 8, HEAD_DIM), f32),
+            pltpu.VMEM((LINE, 2, 8, HEAD_DIM), f32),
             dma((2, N_SHARD)), dma((2,)),
             dma((2, N_CHUNK)), dma((2,)),
             dma((2, N_SHARD)), dma,
             dma((2, N_CHUNK)), dma,
-            dma((16,)), dma,
-            dma((16,)), dma,
+            dma((N_DP,)), dma,
+            dma((2 * N_Z,)), dma,
+            dma((LINE,)), dma,
             dma((2, 3)), dma,
             pltpu.SemaphoreType.REGULAR,
         ],

time: 165 us -> 164 us (level)
  no operation moved by 1% of the time
where the time goes in v4:
time: 164 us
  Pallas kernels  160 us (98%)
  local copies, waits for them, and re-layouts  3.27 us (2%)
    pallas_call x1, Pallas kernels, per_device(): pl.pallas_call(kernel, out_shape=(jax.ShapeDtypeStruct((SEQ_LEN, 2 * HEAD...  160 us

profile of v4, /device:TPU:1, one launch (start us, length us, event | category | flops | bytes accessed | tf_op | source)
XLA Modules:
  0.0 163.7 jit_solution(6800370174122152116)
XLA Ops:
  0.6 159.8 %shard_map.58 = (bf16[2048,256]{1,0:T(8,128)(2,1)S(1)}, bf16[2,3,64,4096]{3,2,1,0:T(8,128)(2,1)S(1)}, f32[3,4096]{1,0:T(4,128)S(1)}) custom-call(bf16[2,3,64,4096]{3,2,1,0:T(8,128)(2,1)} %bitcast.10, f32[3,4096]{1,0:T(4,128)} %bias_hbm.1, bf16[2048,256]{1,0:T(8,128)(2,1)} %bitcast.11), custom_call_target="tpu_custom_call" | custom-call | flops 8000000000 | bytes 10485760 | tf_op jit(solution)/shard_map/pallas_call | solution.py:399
  160.4 1.0 copy.9
  161.4 1.7 %copy.10 = bf16[1,2,64,3,4096]{4,2,3,1,0:T(8,128)(2,1)} copy(bf16[1,2,64,3,4096]{4,2,3,1,0:T(8,128)(2,1)S(1)} %bitcast.8) | data formatting | bytes 6291456
  163.0 0.6 copy.11

commit v5 on v4

--- a/solution.py
+++ b/solution.py
@@ -191,6 +191,7 @@
         pl.semaphore_wait(ready, N_Z)
 
     start_cot(0)
+    start_cot(1)
 
     def follow_in(step, carry):
         in_copy(step, 0).wait_send()
@@ -198,7 +199,6 @@
         return carry
 
     lax.fori_loop(1, N_SHARD, follow_in, 0)
-    start_cot(1)
 
     part[...] = jnp.zeros_like(part)
 

time: 164 us -> 164 us (level)
  no operation moved by 1% of the time
where the time goes in v5:
time: 164 us
  Pallas kernels  160 us (98%)
  local copies, waits for them, and re-layouts  3.27 us (2%)
    pallas_call x1, Pallas kernels, per_device(): pl.pallas_call(kernel, out_shape=(jax.ShapeDtypeStruct((SEQ_LEN, 2 * HEAD...  160 us

profile of v5, /device:TPU:1, one launch (start us, length us, event | category | flops | bytes accessed | tf_op | source)
XLA Modules:
  0.0 163.7 jit_solution(5442805512459754120)
XLA Ops:
  0.6 159.8 %shard_map.58 = (bf16[2048,256]{1,0:T(8,128)(2,1)S(1)}, bf16[2,3,64,4096]{3,2,1,0:T(8,128)(2,1)S(1)}, f32[3,4096]{1,0:T(4,128)S(1)}) custom-call(bf16[2,3,64,4096]{3,2,1,0:T(8,128)(2,1)} %bitcast.10, f32[3,4096]{1,0:T(4,128)} %bias_hbm.1, bf16[2048,256]{1,0:T(8,128)(2,1)} %bitcast.11), custom_call_target="tpu_custom_call" | custom-call | flops 8000000000 | bytes 10485760 | tf_op jit(solution)/shard_map/pallas_call | solution.py:399
  160.4 1.0 copy.9
  161.4 1.7 %copy.10 = bf16[1,2,64,3,4096]{4,2,3,1,0:T(8,128)(2,1)} copy(bf16[1,2,64,3,4096]{4,2,3,1,0:T(8,128)(2,1)S(1)} %bitcast.8) | data formatting | bytes 6291456
  163.0 0.6 copy.11

commit v6 on v5

--- a/solution.py
+++ b/solution.py
@@ -15,8 +15,8 @@
 SEQ_LEN = N_SHARD * PIECE
 WIDTH = 4096
 BLOCK = 512
-SECOND_STAGE = 16
-THIRD_STAGE = 26
+SECOND_STAGE = 12
+THIRD_STAGE = 24
 CHUNK = 512
 N_CHUNK = SEQ_LEN // CHUNK
 N_BLOCK = SEQ_LEN // BLOCK

time: 164 us -> 164 us (level)
  no operation moved by 1% of the time
where the time goes in v6:
time: 164 us
  Pallas kernels  160 us (98%)
  local copies, waits for them, and re-layouts  3.27 us (2%)
    pallas_call x1, Pallas kernels, per_device(): pl.pallas_call(kernel, out_shape=(jax.ShapeDtypeStruct((SEQ_LEN, 2 * HEAD...  160 us

profile of v6, /device:TPU:1, one launch (start us, length us, event | category | flops | bytes accessed | tf_op | source)
XLA Modules:
  0.0 163.6 jit_solution(7919834608518476022)
XLA Ops:
  0.6 159.6 %shard_map.58 = (bf16[2048,256]{1,0:T(8,128)(2,1)S(1)}, bf16[2,3,64,4096]{3,2,1,0:T(8,128)(2,1)S(1)}, f32[3,4096]{1,0:T(4,128)S(1)}) custom-call(bf16[2,3,64,4096]{3,2,1,0:T(8,128)(2,1)} %bitcast.10, f32[3,4096]{1,0:T(4,128)} %bias_hbm.1, bf16[2048,256]{1,0:T(8,128)(2,1)} %bitcast.11), custom_call_target="tpu_custom_call" | custom-call | flops 8000000000 | bytes 10485760 | tf_op jit(solution)/shard_map/pallas_call | solution.py:399
  160.3 1.0 copy.9
  161.3 1.7 %copy.10 = bf16[1,2,64,3,4096]{4,2,3,1,0:T(8,128)(2,1)} copy(bf16[1,2,64,3,4096]{4,2,3,1,0:T(8,128)(2,1)S(1)} %bitcast.8) | data formatting | bytes 6291456
  162.9 0.6 copy.11
